TPU v7x, 256 devices: a whole 4x4x8 slice. The times are simulated.
256 devices in a mesh: lon: 256 (over x, y, z, core).
Axes of the slice: x: 4, y: 4, z: 8, core: 2. Of those that a mesh axis runs over, the one named last changes fastest.
Arguments:
- field: float32 [16, 13312, 200], P(None, 'lon'), may hold values from -6 to 6
- south_rows: float32 [8, 13312, 200], P(None, 'lon'), may hold values from -6 to 6
- sign_mask: int32 [200], replicated, may hold values from -1 to 1, as said below
- weights: float32 [4, 9, 200, 200], replicated, may hold values from -0.125 to 0.125
- biases: float32 [4, 200], replicated, may hold values from -3 to 3
Outputs:
- result: float32 [16, 13312, 200], P(None, 'lon')
Inputs may be any that keep to these rules, and one draw needn't show every extreme that they name: `sign_mask`: every entry is +1 or -1.
All inputs are finite; a program needn't handle non-finite values.
Results may differ from a plain program's by a relative error of at most 0.0001.
Values sent between devices are 32-bit elements; how exact they have to be, the bound alone decides.
A program may use at most 64 MiB of HBM per device.

v0:
```python
import functools

import jax
import jax.numpy as jnp
from jax import lax
from jax.experimental import pallas as pl
from jax.experimental.pallas import tpu as pltpu
from jax.sharding import PartitionSpec as P

MESH = pl.DeviceIdType.MESH
F32 = jnp.float32
BF16 = jnp.bfloat16
R = 16
W = 15


def reverse_rows(v):
    row = lax.broadcasted_iota(jnp.int32, v.shape, 1)
    v = pltpu.roll(v, 4, 1)
    v = jnp.where((row & 2) == 0, pltpu.roll(v, 6, 1), pltpu.roll(v, 2, 1))
    return jnp.where((row & 1) == 0, pltpu.roll(v, 7, 1), pltpu.roll(v, 1, 1))


def gelu(x):
    return 0.5 * x * (1.0 + jnp.tanh(0.7978845608028654 * (x + 0.044715 * (x * x * x))))


def kernel(ndev, n, field, south, sign, weights, bias, out, wf, wh, wl, slab, xh, xl, acc,
           wsem, lsem, ssem, rsem):
    me = lax.axis_index("lon")
    right, left, twin = lax.rem(me + 1, ndev), lax.rem(me + ndev - 1, ndev), ndev - 1 - me
    total = n + 2 * W

    loads = [pltpu.make_async_copy(weights.at[pl.ds(9 * l, 9)], wf.at[pl.ds(9 * l, 9)], wsem.at[l]) for l in range(4)]
    loads[0].start()
    own = [pltpu.make_async_copy(field, slab.at[0, 0, pl.ds(W, n), pl.ds(8, R)], lsem.at[0]),
           pltpu.make_async_copy(south, slab.at[0, 0, pl.ds(W, n), pl.ds(0, 8)], lsem.at[1])]
    for c in own:
        c.start()
    for c in loads[1:]:
        c.start()

    barrier = pltpu.get_barrier_semaphore()
    for peer in (left, right, twin):
        pl.semaphore_signal(barrier, inc=1, device_id=(peer,), device_id_type=MESH)
    pl.semaphore_wait(barrier, 3)

    def remote(src, dst, k, peer):
        return pltpu.make_async_remote_copy(src_ref=src, dst_ref=dst, send_sem=ssem.at[k], recv_sem=rsem.at[k],
                                            device_id=(peer,), device_id_type=MESH)

    fold = [remote(field.at[:, pl.ds(8, 8)], slab.at[1, 0, pl.ds(W, n), pl.ds(16, 8)], 0, twin),
            remote(field.at[:, pl.ds(0, 8)], slab.at[1, 0, pl.ds(W, n), pl.ds(8, 8)], 1, twin)]
    edge = [remote(field.at[pl.ds(n - W, W)], slab.at[0, 0, pl.ds(0, W), pl.ds(8, R)], 2, right),
            remote(field.at[pl.ds(0, W)], slab.at[0, 0, pl.ds(W + n, W), pl.ds(8, R)], 3, left),
            remote(south.at[pl.ds(n - W, W)], slab.at[0, 0, pl.ds(0, W), pl.ds(0, 8)], 4, right),
            remote(south.at[pl.ds(0, W)], slab.at[0, 0, pl.ds(W + n, W), pl.ds(0, 8)], 5, left)]

    def onward(row, k):
        rows = pl.ds(row, 8)
        return [remote(slab.at[1, 0, pl.ds(n, W), rows], slab.at[1, 0, pl.ds(0, W), rows], k, left),
                remote(slab.at[1, 0, pl.ds(W, W), rows], slab.at[1, 0, pl.ds(W + n, W), rows], k + 1, right)]

    upper, lower = onward(16, 6), onward(8, 8)

    fold[0].start()
    for c in edge:
        c.start()
    fold[1].start()

    def prepare(l):
        loads[l].wait()

        def one(t, _):
            w = wf[t]
            hi = w.astype(BF16)
            wh[t] = hi
            wl[t] = (w - hi.astype(F32)).astype(BF16)
            return 0

        lax.fori_loop(9 * l, 9 * l + 9, one, 0)

    def north(side, l):
        def one(j, _):
            v = slab[1 - side, l, pl.ds(total - 2 - 2 * j, 2), pl.ds(16, 8), :]
            v = reverse_rows(v) * sign[...]
            slab[side, l, pl.ds(2 * j, 1), pl.ds(24, 8), :] = v[1:2]
            slab[side, l, pl.ds(2 * j + 1, 1), pl.ds(24, 8), :] = v[0:1]
            return 0

        lax.fori_loop(0, total // 2, one, 0)

    def layer(l, first, second, cols):
        s = 2 ** l
        for a in range(3):
            def part(window):
                side, row, col = window
                return slab[side, l, pl.ds(col - s, cols + 2 * s), pl.ds(row + (a - 1) * s, 8), :]

            x = jnp.concatenate([part(first), part(second)], axis=1)
            hi = x.astype(BF16)
            xh[a, pl.ds(0, cols + 2 * s)] = hi
            xl[a, pl.ds(0, cols + 2 * s)] = (x - hi.astype(F32)).astype(BF16)
        size = cols * R

        def tap(i, _):
            a, b = i // 3, i % 3
            rows = pl.ds(b * s, cols)
            h = xh[a, rows].reshape(size, -1)
            lo = xl[a, rows].reshape(size, -1)
            t = 9 * l + i
            d = jnp.dot(h, wh[t], preferred_element_type=F32)
            d += jnp.dot(lo, wh[t], preferred_element_type=F32)
            d += jnp.dot(h, wl[t], preferred_element_type=F32)
            acc[pl.ds(0, size)] += d
            return 0

        acc[pl.ds(0, size)] = jnp.broadcast_to(bias[pl.ds(l, 1)], (size, acc.shape[-1]))
        lax.fori_loop(0, 9, tap, 0)
        g = gelu(acc[pl.ds(0, size)]).reshape(cols, R, -1)
        for window, lo_row in ((first, 0), (second, 8)):
            side, row, col = window
            new = slab[side, l, pl.ds(col, cols), pl.ds(row, 8), :] + g[:, lo_row:lo_row + 8]
            if l == 3:
                out[pl.ds(col - W, cols), pl.ds(row - 8, 8), :] = new
            else:
                slab[side, l + 1, pl.ds(col, cols), pl.ds(row, 8), :] = new

    zero = jnp.zeros((total, 8, slab.shape[-1]), F32)
    slab[1, 0, :, pl.ds(0, 8), :] = zero
    for l in range(4):
        prepare(l)
    for c in own:
        c.wait()
    for c in edge:
        c.wait()
    for l in range(1, 4):
        slab[0, l, :, pl.ds(0, 8), :] = slab[0, 0, :, pl.ds(0, 8), :]
        slab[1, l, :, pl.ds(0, 8), :] = zero

    low, high = (0, 8), (0, 16)
    fold[0].wait()
    for c in upper:
        c.start()
    for c in upper:
        c.wait()
    fold[1].wait()
    for c in lower:
        c.start()
    for c in lower:
        c.wait()
    c1, c2, c3 = 1, 3, 7
    n1, n2, n3 = total - 2, total - 6, total - 14
    north(0, 0)
    north(1, 0)
    layer(0, (0, 8, c1), (0, 16, c1), n1)
    layer(0, (1, 8, c1), (1, 16, c1), n1)
    north(0, 1)
    north(1, 1)
    layer(1, (0, 8, c2), (0, 16, c2), n2)
    layer(1, (1, 8, c2), (1, 16, c2), n2)
    north(0, 2)
    north(1, 2)
    layer(2, (0, 8, c3), (0, 16, c3), n3)
    layer(2, (1, 16, c3), (1, 16, c3 + n3 // 2), n3 // 2)
    north(0, 3)
    layer(3, (0, 8, W), (0, 16, W), n)


def local(ndev, field, south, sign, weights, bias):
    rows, n, c = field.shape
    total = n + 2 * W
    weights = weights.reshape(-1, c, c)
    taps = weights.shape[0]
    any_ = pl.BlockSpec(memory_space=pl.ANY)
    vmem = pl.BlockSpec(memory_space=pltpu.VMEM)
    result = pl.pallas_call(
        functools.partial(kernel, ndev, n),
        out_shape=jax.ShapeDtypeStruct((n, rows, c), F32),
        in_specs=[any_, any_, vmem, any_, vmem],
        out_specs=vmem,
        scratch_shapes=[
            pltpu.VMEM((taps, c, c), F32),
            pltpu.VMEM((taps, c, c), BF16),
            pltpu.VMEM((taps, c, c), BF16),
            pltpu.VMEM((2, 4, total, 32, c), F32),
            pltpu.VMEM((3, total, R, c), BF16),
            pltpu.VMEM((3, total, R, c), BF16),
            pltpu.VMEM(((total - 2) * R, c), F32),
            pltpu.SemaphoreType.DMA((4,)),
            pltpu.SemaphoreType.DMA((2,)),
            pltpu.SemaphoreType.DMA((10,)),
            pltpu.SemaphoreType.DMA((10,)),
        ],
        compiler_params=pltpu.CompilerParams(collective_id=0, has_side_effects=True, vmem_limit_bytes=60 << 20),
    )(field.transpose(1, 0, 2), south.transpose(1, 0, 2), sign.astype(F32).reshape(1, -1), weights, bias)
    return result.transpose(1, 0, 2)


def solution(mesh):
    ndev = mesh.shape["lon"]
    lon = P(None, "lon", None)
    return jax.shard_map(functools.partial(local, ndev), mesh=mesh, in_specs=(lon, lon, P(), P(), P()),
                         out_specs=lon, check_vma=False)
```

profile of v0, /device:TPU:0, one launch (start us, length us, event | category | flops | bytes accessed | tf_op | source)
XLA Modules:
  0.0 114.2 jit_solution(9281797397468227508)
XLA Ops:
  0.0 1.2 %convert_element_type.3 = f32[200]{0:T(256)} convert(s32[200]{0:T(256)} %param.7) | non-fusion elementwise | flops 200 | bytes 1600 | tf_op jit(solution)/shard_map/convert_element_type | solution.py:196
  1.2 110.8 %shard_map.55 = f32[52,16,200]{2,1,0:T(8,128)} custom-call(f32[52,16,200]{2,1,0:T(8,128)} %bitcast.7, f32[52,8,200]{2,1,0:T(8,128)} %bitcast.8, f32[1,200]{1,0:T(1,128)} %bitcast.9, f32[36,200,200]{2,1,0:T(8,128)} %bitcast.5, f32[4,200]{1,0:T(4,128)} %bias.1), custom_call_target="tpu_custom_call" | custom-call | tf_op jit(solution)/shard_map/pallas_call | solution.py:177
  112.1 2.1 %copy.7 = f32[16,52,200]{2,0,1:T(8,128)} copy(f32[16,52,200]{2,0,1:T(8,128)} %bitcast.6) | data formatting | bytes 1331200
where the time goes:
time: 114 us
  Pallas kernels  111 us (97%)
  local copies, waits for them, and re-layouts  2.11 us (2%)
  other arithmetic  1.24 us (1%)
    pallas_call x1, Pallas kernels, local(): pl.pallas_call(functools.partial(kernel, ndev, n), out_shape=jax.ShapeDty...  111 us

commit v1 on v0

--- a/solution.py
+++ b/solution.py
@@ -11,6 +11,7 @@
 F32 = jnp.float32
 BF16 = jnp.bfloat16
 R = 16
+PIECE = 20
 W = 15
 
 
@@ -25,7 +26,7 @@
     return 0.5 * x * (1.0 + jnp.tanh(0.7978845608028654 * (x + 0.044715 * (x * x * x))))
 
 
-def kernel(ndev, n, field, south, sign, weights, bias, out, wf, wh, wl, slab, xh, xl, acc,
+def kernel(ndev, n, field, south, sign, weights, bias, out, wf, wh, wl, slab, xh, xl, gain,
            wsem, lsem, ssem, rsem):
     me = lax.axis_index("lon")
     right, left, twin = lax.rem(me + 1, ndev), lax.rem(me + ndev - 1, ndev), ndev - 1 - me
@@ -80,91 +81,154 @@
 
         lax.fori_loop(9 * l, 9 * l + 9, one, 0)
 
+    def group(count):
+        return 4 if count % 4 == 0 else 3 if count % 3 == 0 else 2
+
     def north(side, l):
+        first = 2 ** l - 1
+        count = total - 2 * first
+        g = group(count)
+
         def one(j, _):
-            v = slab[1 - side, l, pl.ds(total - 2 - 2 * j, 2), pl.ds(16, 8), :]
+            start = first + g * j
+            v = slab[1 - side, l, pl.ds(total - g - start, g), pl.ds(16, 8), :]
             v = reverse_rows(v) * sign[...]
-            slab[side, l, pl.ds(2 * j, 1), pl.ds(24, 8), :] = v[1:2]
-            slab[side, l, pl.ds(2 * j + 1, 1), pl.ds(24, 8), :] = v[0:1]
-            return 0
-
-        lax.fori_loop(0, total // 2, one, 0)
-
-    def layer(l, first, second, cols):
+            for k in range(g):
+                slab[side, l, pl.ds(start + k, 1), pl.ds(24, 8), :] = v[g - 1 - k:g - k]
+            return 0
+
+        lax.fori_loop(0, count // g, one, 0)
+
+    def build(l, windows, cols):
         s = 2 ** l
-        for a in range(3):
-            def part(window):
-                side, row, col = window
-                return slab[side, l, pl.ds(col - s, cols + 2 * s), pl.ds(row + (a - 1) * s, 8), :]
-
-            x = jnp.concatenate([part(first), part(second)], axis=1)
-            hi = x.astype(BF16)
-            xh[a, pl.ds(0, cols + 2 * s)] = hi
-            xl[a, pl.ds(0, cols + 2 * s)] = (x - hi.astype(F32)).astype(BF16)
-        size = cols * R
-
-        def tap(i, _):
+        count = cols + 2 * s
+        g = group(count)
+
+        def one(j, _):
+            for a in range(3):
+                x = jnp.concatenate([slab[side, l, pl.ds(col - s + g * j, g), pl.ds(row + (a - 1) * s, 8), :]
+                                     for side, row, col in windows], axis=1)
+                hi = x.astype(BF16)
+                xh[a, pl.ds(g * j, g)] = hi
+                xl[a, pl.ds(g * j, g)] = (x - hi.astype(F32)).astype(BF16)
+            return 0
+
+        lax.fori_loop(0, count // g, one, 0)
+
+    def update(l, windows, cols):
+        g = group(cols)
+
+        def one(j, _):
+            for k, (side, row, col) in enumerate(windows):
+                place = pl.ds(col + g * j, g)
+                new = slab[side, l, place, pl.ds(row, 8), :] + gain[pl.ds(g * j, g), pl.ds(8 * k, 8), :]
+                if l == 3:
+                    out[pl.ds(col - W + g * j, g), pl.ds(row - 8, 8), :] = new
+                else:
+                    slab[side, l + 1, place, pl.ds(row, 8), :] = new
+            return 0
+
+        lax.fori_loop(0, cols // g, one, 0)
+
+    def chunk(l, s, start):
+        d = None
+        for i in range(9):
             a, b = i // 3, i % 3
-            rows = pl.ds(b * s, cols)
-            h = xh[a, rows].reshape(size, -1)
-            lo = xl[a, rows].reshape(size, -1)
-            t = 9 * l + i
-            d = jnp.dot(h, wh[t], preferred_element_type=F32)
-            d += jnp.dot(lo, wh[t], preferred_element_type=F32)
-            d += jnp.dot(h, wl[t], preferred_element_type=F32)
-            acc[pl.ds(0, size)] += d
-            return 0
-
-        acc[pl.ds(0, size)] = jnp.broadcast_to(bias[pl.ds(l, 1)], (size, acc.shape[-1]))
-        lax.fori_loop(0, 9, tap, 0)
-        g = gelu(acc[pl.ds(0, size)]).reshape(cols, R, -1)
-        for window, lo_row in ((first, 0), (second, 8)):
-            side, row, col = window
-            new = slab[side, l, pl.ds(col, cols), pl.ds(row, 8), :] + g[:, lo_row:lo_row + 8]
-            if l == 3:
-                out[pl.ds(col - W, cols), pl.ds(row - 8, 8), :] = new
-            else:
-                slab[side, l + 1, pl.ds(col, cols), pl.ds(row, 8), :] = new
+            rows = pl.ds(start + b * s, PIECE)
+            h = xh[a, rows].reshape(PIECE * R, -1)
+            lo = xl[a, rows].reshape(PIECE * R, -1)
+            for x, w in ((h, wh), (lo, wh), (h, wl)):
+                e = jnp.dot(x, w[9 * l + i], preferred_element_type=F32)
+                d = e if d is None else d + e
+        gain[pl.ds(start, PIECE)] = gelu(d + bias[pl.ds(l, 1)]).reshape(PIECE, R, -1)
+
+    c1, c2, c3 = 1, 3, 7
+    n1, n2, n3 = total - 2, total - 6, total - 14
+    S8, S16, M16 = (0, 8), (0, 16), (1, 16)
+
+    def pair(x, y, c):
+        return [x + (c,), y + (c,)]
+
+    def halves(x, c, m):
+        return [x + (c,), x + (c + m // 2,)]
+
+    def start_all(copies):
+        for c in copies:
+            c.start()
+
+    def wait_all(copies):
+        for c in copies:
+            c.wait()
+
+    def first():
+        wait_all(own)
+        wait_all(edge)
+        for l in range(1, 4):
+            slab[0, l, :, pl.ds(0, 8), :] = slab[0, 0, :, pl.ds(0, 8), :]
+            slab[1, l, :, pl.ds(0, 8), :] = zero
+
+    def upper_sent():
+        fold[0].wait()
+        start_all(upper)
+
+    def upper_here():
+        wait_all(upper)
+        north(0, 0)
+        north(1, 0)
+
+    def lower_sent():
+        fold[1].wait()
+        start_all(lower)
+        north(0, 2)
+
+    def lower_here():
+        wait_all(lower)
+        north(1, 2)
+
+    steps = [
+        (0, pair(S8, S16, c1), n1, first),
+        (1, pair(S8, S16, c2), n2, None),
+        (2, halves(S8, c3, n3), n3 // 2, upper_sent),
+        (0, pair(S16, (1, 17), c1), n1, upper_here),
+        (1, pair(S16, M16, c2), n2, lambda: (north(0, 1), north(1, 1))),
+        (2, halves(S16, c3, n3), n3 // 2, lower_sent),
+        (0, halves((1, 9), c1, n1), n1 // 2, lower_here),
+        (1, halves((1, 12), c2, n2), n2 // 2, None),
+        (2, halves(M16, c3, n3), n3 // 2, None),
+        (3, pair(S8, S16, W), n, lambda: north(0, 3)),
+    ]
 
     zero = jnp.zeros((total, 8, slab.shape[-1]), F32)
     slab[1, 0, :, pl.ds(0, 8), :] = zero
     for l in range(4):
         prepare(l)
-    for c in own:
-        c.wait()
-    for c in edge:
-        c.wait()
-    for l in range(1, 4):
-        slab[0, l, :, pl.ds(0, 8), :] = slab[0, 0, :, pl.ds(0, 8), :]
-        slab[1, l, :, pl.ds(0, 8), :] = zero
-
-    low, high = (0, 8), (0, 16)
-    fold[0].wait()
-    for c in upper:
-        c.start()
-    for c in upper:
-        c.wait()
-    fold[1].wait()
-    for c in lower:
-        c.start()
-    for c in lower:
-        c.wait()
-    c1, c2, c3 = 1, 3, 7
-    n1, n2, n3 = total - 2, total - 6, total - 14
-    north(0, 0)
-    north(1, 0)
-    layer(0, (0, 8, c1), (0, 16, c1), n1)
-    layer(0, (1, 8, c1), (1, 16, c1), n1)
-    north(0, 1)
-    north(1, 1)
-    layer(1, (0, 8, c2), (0, 16, c2), n2)
-    layer(1, (1, 8, c2), (1, 16, c2), n2)
-    north(0, 2)
-    north(1, 2)
-    layer(2, (0, 8, c3), (0, 16, c3), n3)
-    layer(2, (1, 16, c3), (1, 16, c3 + n3 // 2), n3 // 2)
-    north(0, 3)
-    layer(3, (0, 8, W), (0, 16, W), n)
+
+    def step(p, _):
+        l = jnp.int32(0)
+        cols = jnp.int32(0)
+        for k, (layer, windows, count, before) in enumerate(steps):
+            @pl.when(p == k)
+            def _():
+                if before is not None:
+                    before()
+                build(layer, windows, count)
+
+            l = jnp.where(p == k, layer, l)
+            cols = jnp.where(p == k, count, cols)
+        s = jnp.where(l == 0, 1, jnp.where(l == 1, 2, jnp.where(l == 2, 4, 8)))
+
+        def one(q, _):
+            chunk(l, s, jnp.minimum(q * PIECE, cols - PIECE))
+            return 0
+
+        lax.fori_loop(0, (cols + PIECE - 1) // PIECE, one, 0)
+        for k, (layer, windows, count, before) in enumerate(steps):
+            @pl.when(p == k)
+            def _():
+                update(layer, windows, count)
+        return 0
+
+    lax.fori_loop(0, len(steps), step, 0)
 
 
 def local(ndev, field, south, sign, weights, bias):
@@ -186,7 +250,7 @@
             pltpu.VMEM((2, 4, total, 32, c), F32),
             pltpu.VMEM((3, total, R, c), BF16),
             pltpu.VMEM((3, total, R, c), BF16),
-            pltpu.VMEM(((total - 2) * R, c), F32),
+            pltpu.VMEM((total, R, c), F32),
             pltpu.SemaphoreType.DMA((4,)),
             pltpu.SemaphoreType.DMA((2,)),
             pltpu.SemaphoreType.DMA((10,)),

time: 114 us -> 108 us (0.947)
  Pallas kernels: 111 us -> 104 us
    pallas_call x1, Pallas kernels: 111 us -> 104 us  [local(): pl.pallas_call(functools.partial(kernel, ndev, n), out_shape=jax.ShapeDty...]
where the time goes in v1:
time: 108 us; the launch traced here: 107 us
  Pallas kernels  104 us (96%)
  local copies, waits for them, and re-layouts  2.11 us (2%)
  other arithmetic  1.24 us (1%)
    pallas_call x1, Pallas kernels, local(): pl.pallas_call(functools.partial(kernel, ndev, n), out_shape=jax.ShapeDty...  104 us

profile of v1, /device:TPU:0, one launch (start us, length us, event | category | flops | bytes accessed | tf_op | source)
XLA Modules:
  0.0 107.3 jit_solution(1246764262433469554)
XLA Ops:
  0.0 1.2 %convert_element_type.3 = f32[200]{0:T(256)} convert(s32[200]{0:T(256)} %param.7) | non-fusion elementwise | flops 200 | bytes 1600 | tf_op jit(solution)/shard_map/convert_element_type | solution.py:260
  1.2 103.9 %shard_map.55 = f32[52,16,200]{2,1,0:T(8,128)} custom-call(f32[52,16,200]{2,1,0:T(8,128)} %bitcast.7, f32[52,8,200]{2,1,0:T(8,128)} %bitcast.8, f32[1,200]{1,0:T(1,128)} %bitcast.9, f32[36,200,200]{2,1,0:T(8,128)} %bitcast.5, f32[4,200]{1,0:T(4,128)} %bias.1), custom_call_target="tpu_custom_call" | custom-call | tf_op jit(solution)/shard_map/pallas_call | solution.py:241
  105.2 2.1 %copy.7 = f32[16,52,200]{2,0,1:T(8,128)} copy(f32[16,52,200]{2,0,1:T(8,128)} %bitcast.6) | data formatting | bytes 1331200

commit v2 on v1

--- a/solution.py
+++ b/solution.py
@@ -12,6 +12,7 @@
 BF16 = jnp.bfloat16
 R = 16
 PIECE = 20
+LANES = 128
 W = 15
 
 
@@ -22,15 +23,34 @@
     return jnp.where((row & 1) == 0, pltpu.roll(v, 7, 1), pltpu.roll(v, 1, 1))
 
 
+def parcels(n, c):
+    tail = c - LANES - 64
+    share = LANES // tail
+    parts, spans, first = [], [], 0
+    for columns in (list(range(W)) + list(range(n - W, n)), list(range(W, n - W))):
+        half = len(columns) // 2
+        pairs = list(zip(columns[:half], columns[half:]))
+        rests = [columns[k:k + share] for k in range(0, len(columns), share)]
+        count = len(columns) + half + len(rests)
+        parts.append((first, columns, pairs, rests))
+        spans.append((first, count))
+        first += count
+    return parts, spans
+
+
 def gelu(x):
     return 0.5 * x * (1.0 + jnp.tanh(0.7978845608028654 * (x + 0.044715 * (x * x * x))))
 
 
-def kernel(ndev, n, field, south, sign, weights, bias, out, wf, wh, wl, slab, xh, xl, gain,
+def kernel(ndev, n, field, south, sign, weights, bias, out, wf, wh, wl, slab, xh, xl, gain, raw, parcel, landed,
            wsem, lsem, ssem, rsem):
     me = lax.axis_index("lon")
     right, left, twin = lax.rem(me + 1, ndev), lax.rem(me + ndev - 1, ndev), ndev - 1 - me
     total = n + 2 * W
+
+    barrier = pltpu.get_barrier_semaphore()
+    for peer in (left, right, twin):
+        pl.semaphore_signal(barrier, inc=1, device_id=(peer,), device_id_type=MESH)
 
     loads = [pltpu.make_async_copy(weights.at[pl.ds(9 * l, 9)], wf.at[pl.ds(9 * l, 9)], wsem.at[l]) for l in range(4)]
     loads[0].start()
@@ -41,17 +61,62 @@
     for c in loads[1:]:
         c.start()
 
-    barrier = pltpu.get_barrier_semaphore()
-    for peer in (left, right, twin):
-        pl.semaphore_signal(barrier, inc=1, device_id=(peer,), device_id_type=MESH)
-    pl.semaphore_wait(barrier, 3)
-
     def remote(src, dst, k, peer):
         return pltpu.make_async_remote_copy(src_ref=src, dst_ref=dst, send_sem=ssem.at[k], recv_sem=rsem.at[k],
                                             device_id=(peer,), device_id_type=MESH)
 
-    fold = [remote(field.at[:, pl.ds(8, 8)], slab.at[1, 0, pl.ds(W, n), pl.ds(16, 8)], 0, twin),
-            remote(field.at[:, pl.ds(0, 8)], slab.at[1, 0, pl.ds(W, n), pl.ds(8, 8)], 1, twin)]
+    parts, spans = parcels(n, field.shape[-1])
+    tail = field.shape[-1] - LANES - 64
+
+    def pack(half):
+        rows = pl.ds(16 - 8 * half, 8)
+        lane = lax.broadcasted_iota(jnp.int32, (8, LANES), 1)
+        blank = jnp.zeros((8, LANES - 64 - tail), F32)
+
+        def upper_lanes(j):
+            return jnp.concatenate([slab[0, 0, W + j, rows, LANES:], blank], axis=1)
+
+        for first, columns, pairs, rests in parts:
+            t = first
+            for j in columns:
+                parcel[half, t] = slab[0, 0, W + j, rows, :LANES]
+                t += 1
+            for j, k in pairs:
+                parcel[half, t] = jnp.where(lane < 64, upper_lanes(j), pltpu.roll(upper_lanes(k), 64, 1))
+                t += 1
+            for some in rests:
+                v = pltpu.roll(upper_lanes(some[0]), 64, 1)
+                for k, j in enumerate(some[1:], 1):
+                    v = jnp.where(lane < tail * k, v, pltpu.roll(upper_lanes(j), (64 + tail * k) % LANES, 1))
+                parcel[half, t] = v
+                t += 1
+
+    def unpack(half, part):
+        rows = pl.ds(16 - 8 * half, 8)
+        lane = lax.broadcasted_iota(jnp.int32, (8, LANES), 1)
+        first, columns, pairs, rests = parts[part]
+        t = first
+        for j in columns:
+            slab[1, 0, W + j, rows, :LANES] = landed[half, t]
+            t += 1
+        wide = {}
+        for pair in pairs:
+            v = landed[half, t]
+            wide[pair[0]], wide[pair[1]] = v, pltpu.roll(v, 64, 1)
+            t += 1
+        for some in rests:
+            v = landed[half, t]
+            for k, j in enumerate(some):
+                last = pltpu.roll(v, (64 - tail * k) % LANES, 1)
+                slab[1, 0, W + j, rows, LANES:] = jnp.where(lane < 64, wide[j], last)[:, :64 + tail]
+            t += 1
+
+    def parcel_copy(half, part, k):
+        first, count = spans[part]
+        place = (half, pl.ds(first, count), pl.ds(half, 8 - half))
+        return remote(parcel.at[place], landed.at[place], k, twin)
+
+    fold = [[parcel_copy(half, part, (0, 1, 10, 11)[2 * half + part]) for part in range(2)] for half in range(2)]
     edge = [remote(field.at[pl.ds(n - W, W)], slab.at[0, 0, pl.ds(0, W), pl.ds(8, R)], 2, right),
             remote(field.at[pl.ds(0, W)], slab.at[0, 0, pl.ds(W + n, W), pl.ds(8, R)], 3, left),
             remote(south.at[pl.ds(n - W, W)], slab.at[0, 0, pl.ds(0, W), pl.ds(0, 8)], 4, right),
@@ -64,10 +129,16 @@
 
     upper, lower = onward(16, 6), onward(8, 8)
 
-    fold[0].start()
+    own[0].wait()
+    pack(0)
+    pack(1)
+    pl.semaphore_wait(barrier, 3)
     for c in edge:
         c.start()
-    fold[1].start()
+    for c in fold[0]:
+        c.start()
+    for c in fold[1]:
+        c.start()
 
     def prepare(l):
         loads[l].wait()
@@ -130,7 +201,7 @@
 
         lax.fori_loop(0, cols // g, one, 0)
 
-    def chunk(l, s, start):
+    def chunk(l, s, start, slot):
         d = None
         for i in range(9):
             a, b = i // 3, i % 3
@@ -140,7 +211,10 @@
             for x, w in ((h, wh), (lo, wh), (h, wl)):
                 e = jnp.dot(x, w[9 * l + i], preferred_element_type=F32)
                 d = e if d is None else d + e
-        gain[pl.ds(start, PIECE)] = gelu(d + bias[pl.ds(l, 1)]).reshape(PIECE, R, -1)
+        raw[slot] = d
+
+    def finish(l, start, slot):
+        gain[pl.ds(start, PIECE)] = gelu(raw[slot] + bias[pl.ds(l, 1)]).reshape(PIECE, R, -1)
 
     c1, c2, c3 = 1, 3, 7
     n1, n2, n3 = total - 2, total - 6, total - 14
@@ -161,27 +235,33 @@
             c.wait()
 
     def first():
-        wait_all(own)
+        own[1].wait()
         wait_all(edge)
         for l in range(1, 4):
             slab[0, l, :, pl.ds(0, 8), :] = slab[0, 0, :, pl.ds(0, 8), :]
             slab[1, l, :, pl.ds(0, 8), :] = zero
 
     def upper_sent():
-        fold[0].wait()
+        fold[0][0].wait()
+        unpack(0, 0)
         start_all(upper)
 
     def upper_here():
+        fold[0][1].wait()
+        unpack(0, 1)
         wait_all(upper)
         north(0, 0)
         north(1, 0)
 
     def lower_sent():
-        fold[1].wait()
+        fold[1][0].wait()
+        unpack(1, 0)
         start_all(lower)
         north(0, 2)
 
     def lower_here():
+        fold[1][1].wait()
+        unpack(1, 1)
         wait_all(lower)
         north(1, 2)
 
@@ -217,11 +297,18 @@
             cols = jnp.where(p == k, count, cols)
         s = jnp.where(l == 0, 1, jnp.where(l == 1, 2, jnp.where(l == 2, 4, 8)))
 
+        pieces = (cols + PIECE - 1) // PIECE
+
+        def place(q):
+            return jnp.maximum(jnp.minimum(q * PIECE, cols - PIECE), 0)
+
         def one(q, _):
-            chunk(l, s, jnp.minimum(q * PIECE, cols - PIECE))
-            return 0
-
-        lax.fori_loop(0, (cols + PIECE - 1) // PIECE, one, 0)
+            finish(l, place(q - 1), (q + 1) % 2)
+            chunk(l, s, place(q), q % 2)
+            return 0
+
+        lax.fori_loop(0, pieces, one, 0)
+        finish(l, place(pieces - 1), (pieces + 1) % 2)
         for k, (layer, windows, count, before) in enumerate(steps):
             @pl.when(p == k)
             def _():
@@ -235,6 +322,7 @@
     rows, n, c = field.shape
     total = n + 2 * W
     weights = weights.reshape(-1, c, c)
+    tiles = sum(count for _, count in parcels(n, c)[1])
     taps = weights.shape[0]
     any_ = pl.BlockSpec(memory_space=pl.ANY)
     vmem = pl.BlockSpec(memory_space=pltpu.VMEM)
@@ -251,10 +339,13 @@
             pltpu.VMEM((3, total, R, c), BF16),
             pltpu.VMEM((3, total, R, c), BF16),
             pltpu.VMEM((total, R, c), F32),
+            pltpu.VMEM((2, PIECE * R, c), F32),
+            pltpu.VMEM((2, tiles, 8, LANES), F32),
+            pltpu.VMEM((2, tiles, 8, LANES), F32),
             pltpu.SemaphoreType.DMA((4,)),
             pltpu.SemaphoreType.DMA((2,)),
-            pltpu.SemaphoreType.DMA((10,)),
-            pltpu.SemaphoreType.DMA((10,)),
+            pltpu.SemaphoreType.DMA((12,)),
+            pltpu.SemaphoreType.DMA((12,)),
         ],
         compiler_params=pltpu.CompilerParams(collective_id=0, has_side_effects=True, vmem_limit_bytes=60 << 20),
     )(field.transpose(1, 0, 2), south.transpose(1, 0, 2), sign.astype(F32).reshape(1, -1), weights, bias)

time: 108 us -> 94.7 us (0.88)
  Pallas kernels: 104 us -> 91.2 us
    pallas_call x1, Pallas kernels: 104 us -> 91.2 us  [local(): pl.pallas_call(functools.partial(kernel, ndev, n), out_shape=jax.ShapeDty...]
where the time goes in v2:
time: 94.7 us; the launch traced here: 94.5 us
  Pallas kernels  91.2 us (96%)
  local copies, waits for them, and re-layouts  2.11 us (2%)
  other arithmetic  1.24 us (1%)
    pallas_call x1, Pallas kernels, local(): pl.pallas_call(functools.partial(kernel, ndev, n), out_shape=jax.ShapeDty...  91.2 us
    unnamed x1, local copies, waits for them, and re-layouts  2.11 us

profile of v2, /device:TPU:0, one launch (start us, length us, event | category | flops | bytes accessed | tf_op | source)
XLA Modules:
  0.0 94.5 jit_solution(8235078939208470348)
XLA Ops:
  0.0 1.2 %convert_element_type.3 = f32[200]{0:T(256)} convert(s32[200]{0:T(256)} %param.7) | non-fusion elementwise | flops 200 | bytes 1600 | tf_op jit(solution)/shard_map/convert_element_type | solution.py:351
  1.2 91.2 %shard_map.55 = f32[52,16,200]{2,1,0:T(8,128)} custom-call(f32[52,16,200]{2,1,0:T(8,128)} %bitcast.7, f32[52,8,200]{2,1,0:T(8,128)} %bitcast.8, f32[1,200]{1,0:T(1,128)} %bitcast.9, f32[36,200,200]{2,1,0:T(8,128)} %bitcast.5, f32[4,200]{1,0:T(4,128)} %bias.1), custom_call_target="tpu_custom_call" | custom-call | tf_op jit(solution)/shard_map/pallas_call | solution.py:329
  92.4 2.1 %copy.7 = f32[16,52,200]{2,0,1:T(8,128)} copy(f32[16,52,200]{2,0,1:T(8,128)} %bitcast.6) | data formatting | bytes 1331200

commit v3 on v2

--- a/solution.py
+++ b/solution.py
@@ -11,6 +11,7 @@
 F32 = jnp.float32
 BF16 = jnp.bfloat16
 R = 16
+MOST = 4
 PIECE = 20
 LANES = 128
 W = 15
@@ -137,8 +138,6 @@
         c.start()
     for c in fold[0]:
         c.start()
-    for c in fold[1]:
-        c.start()
 
     def prepare(l):
         loads[l].wait()
@@ -153,7 +152,7 @@
         lax.fori_loop(9 * l, 9 * l + 9, one, 0)
 
     def group(count):
-        return 4 if count % 4 == 0 else 3 if count % 3 == 0 else 2
+        return max(g for g in range(1, MOST + 1) if count % g == 0)
 
     def north(side, l):
         first = 2 ** l - 1
@@ -170,7 +169,7 @@
 
         lax.fori_loop(0, count // g, one, 0)
 
-    def build(l, windows, cols):
+    def build(l, windows, cols, at):
         s = 2 ** l
         count = cols + 2 * s
         g = group(count)
@@ -180,19 +179,19 @@
                 x = jnp.concatenate([slab[side, l, pl.ds(col - s + g * j, g), pl.ds(row + (a - 1) * s, 8), :]
                                      for side, row, col in windows], axis=1)
                 hi = x.astype(BF16)
-                xh[a, pl.ds(g * j, g)] = hi
-                xl[a, pl.ds(g * j, g)] = (x - hi.astype(F32)).astype(BF16)
+                xh[a, pl.ds(at + g * j, g)] = hi
+                xl[a, pl.ds(at + g * j, g)] = (x - hi.astype(F32)).astype(BF16)
             return 0
 
         lax.fori_loop(0, count // g, one, 0)
 
-    def update(l, windows, cols):
+    def update(l, windows, cols, at):
         g = group(cols)
 
         def one(j, _):
             for k, (side, row, col) in enumerate(windows):
                 place = pl.ds(col + g * j, g)
-                new = slab[side, l, place, pl.ds(row, 8), :] + gain[pl.ds(g * j, g), pl.ds(8 * k, 8), :]
+                new = slab[side, l, place, pl.ds(row, 8), :] + gain[pl.ds(at + g * j, g), pl.ds(8 * k, 8), :]
                 if l == 3:
                     out[pl.ds(col - W + g * j, g), pl.ds(row - 8, 8), :] = new
                 else:
@@ -234,17 +233,26 @@
         for c in copies:
             c.wait()
 
+    def south_rows(cols):
+        for l in range(1, 4):
+            slab[0, l, cols, pl.ds(0, 8), :] = slab[0, 0, cols, pl.ds(0, 8), :]
+
     def first():
         own[1].wait()
+        south_rows(pl.ds(W, n))
+        for l in range(1, 4):
+            slab[1, l, :, pl.ds(0, 8), :] = zero
+
+    def halo_here():
         wait_all(edge)
-        for l in range(1, 4):
-            slab[0, l, :, pl.ds(0, 8), :] = slab[0, 0, :, pl.ds(0, 8), :]
-            slab[1, l, :, pl.ds(0, 8), :] = zero
+        south_rows(pl.ds(0, W))
+        south_rows(pl.ds(W + n, W))
 
     def upper_sent():
         fold[0][0].wait()
         unpack(0, 0)
         start_all(upper)
+        start_all(fold[1])
 
     def upper_here():
         fold[0][1].wait()
@@ -265,18 +273,34 @@
         wait_all(lower)
         north(1, 2)
 
+    def split(layer, c, m):
+        middle = n - 2 * c
+        return ([(pair(S8, S16, W + c), middle)],
+                [(pair(S8, S16, c), W), (pair(S8, S16, W + c + middle), W)])
+
+    middle0, sides0 = split(0, c1, n1)
+    middle1, sides1 = split(1, c2, n2)
     steps = [
-        (0, pair(S8, S16, c1), n1, first),
-        (1, pair(S8, S16, c2), n2, None),
-        (2, halves(S8, c3, n3), n3 // 2, upper_sent),
-        (0, pair(S16, (1, 17), c1), n1, upper_here),
-        (1, pair(S16, M16, c2), n2, lambda: (north(0, 1), north(1, 1))),
-        (2, halves(S16, c3, n3), n3 // 2, lower_sent),
-        (0, halves((1, 9), c1, n1), n1 // 2, lower_here),
-        (1, halves((1, 12), c2, n2), n2 // 2, None),
-        (2, halves(M16, c3, n3), n3 // 2, None),
-        (3, pair(S8, S16, W), n, lambda: north(0, 3)),
+        (0, middle0, first),
+        (1, middle1, None),
+        (0, sides0, halo_here),
+        (1, sides1, None),
+        (2, [(halves(S8, c3, n3), n3 // 2)], upper_sent),
+        (0, [(pair(S16, (1, 17), c1), n1)], upper_here),
+        (1, [(pair(S16, M16, c2), n2)], lambda: (north(0, 1), north(1, 1))),
+        (2, [(halves(S16, c3, n3), n3 // 2)], lower_sent),
+        (0, [(halves((1, 9), c1, n1), n1 // 2)], lower_here),
+        (1, [(halves((1, 12), c2, n2), n2 // 2)], None),
+        (2, [(halves(M16, c3, n3), n3 // 2)], None),
+        (3, [(pair(S8, S16, W), n)], lambda: north(0, 3)),
     ]
+
+    def placed(layer, segments):
+        at, result = 0, []
+        for windows, count in segments:
+            result.append((windows, count, at))
+            at += count + 2 ** (layer + 1)
+        return result, at - 2 ** (layer + 1)
 
     zero = jnp.zeros((total, 8, slab.shape[-1]), F32)
     slab[1, 0, :, pl.ds(0, 8), :] = zero
@@ -286,15 +310,16 @@
     def step(p, _):
         l = jnp.int32(0)
         cols = jnp.int32(0)
-        for k, (layer, windows, count, before) in enumerate(steps):
+        for k, (layer, segments, before) in enumerate(steps):
             @pl.when(p == k)
             def _():
                 if before is not None:
                     before()
-                build(layer, windows, count)
+                for segment in placed(layer, segments)[0]:
+                    build(layer, *segment)
 
             l = jnp.where(p == k, layer, l)
-            cols = jnp.where(p == k, count, cols)
+            cols = jnp.where(p == k, placed(layer, segments)[1], cols)
         s = jnp.where(l == 0, 1, jnp.where(l == 1, 2, jnp.where(l == 2, 4, 8)))
 
         pieces = (cols + PIECE - 1) // PIECE
@@ -309,10 +334,11 @@
 
         lax.fori_loop(0, pieces, one, 0)
         finish(l, place(pieces - 1), (pieces + 1) % 2)
-        for k, (layer, windows, count, before) in enumerate(steps):
+        for k, (layer, segments, before) in enumerate(steps):
             @pl.when(p == k)
             def _():
-                update(layer, windows, count)
+                for segment in placed(layer, segments)[0]:
+                    update(layer, *segment)
         return 0
 
     lax.fori_loop(0, len(steps), step, 0)

time: 94.7 us -> 84.5 us (0.89)
  Pallas kernels: 91.2 us -> 81 us
    pallas_call x1, Pallas kernels: 91.2 us -> 81 us  [local(): pl.pallas_call(functools.partial(kernel, ndev, n), out_shape=jax.ShapeDty...]
where the time goes in v3:
time: 84.5 us; the launch traced here: 84.3 us
  Pallas kernels  81 us (96%)
  local copies, waits for them, and re-layouts  2.11 us (2%)
  other arithmetic  1.24 us (1%)
    pallas_call x1, Pallas kernels, local(): pl.pallas_call(functools.partial(kernel, ndev, n), out_shape=jax.ShapeDty...  81 us
    unnamed x1, local copies, waits for them, and re-layouts  2.11 us

profile of v3, /device:TPU:0, one launch (start us, length us, event | category | flops | bytes accessed | tf_op | source)
XLA Modules:
  0.0 84.3 jit_solution(17349609226393670952)
XLA Ops:
  0.0 1.2 %convert_element_type.3 = f32[200]{0:T(256)} convert(s32[200]{0:T(256)} %param.7) | non-fusion elementwise | flops 200 | bytes 1600 | tf_op jit(solution)/shard_map/convert_element_type | solution.py:377
  1.2 81.0 %shard_map.55 = f32[52,16,200]{2,1,0:T(8,128)} custom-call(f32[52,16,200]{2,1,0:T(8,128)} %bitcast.7, f32[52,8,200]{2,1,0:T(8,128)} %bitcast.8, f32[1,200]{1,0:T(1,128)} %bitcast.9, f32[36,200,200]{2,1,0:T(8,128)} %bitcast.5, f32[4,200]{1,0:T(4,128)} %bias.1), custom_call_target="tpu_custom_call" | custom-call | tf_op jit(solution)/shard_map/pallas_call | solution.py:355
  82.2 2.1 %copy.7 = f32[16,52,200]{2,0,1:T(8,128)} copy(f32[16,52,200]{2,0,1:T(8,128)} %bitcast.6) | data formatting | bytes 1331200

commit v4 on v3

--- a/solution.py
+++ b/solution.py
@@ -11,8 +11,8 @@
 F32 = jnp.float32
 BF16 = jnp.bfloat16
 R = 16
-MOST = 4
-PIECE = 20
+MOST = 8
+PIECES = (20, 19, 17, 26)
 LANES = 128
 W = 15
 
@@ -200,20 +200,38 @@
 
         lax.fori_loop(0, cols // g, one, 0)
 
-    def chunk(l, s, start, slot):
+    def products(l, start, slot):
+        s, piece = 2 ** l, PIECES[l]
         d = None
         for i in range(9):
             a, b = i // 3, i % 3
-            rows = pl.ds(start + b * s, PIECE)
-            h = xh[a, rows].reshape(PIECE * R, -1)
-            lo = xl[a, rows].reshape(PIECE * R, -1)
+            rows = pl.ds(start + b * s, piece)
+            h = xh[a, rows].reshape(piece * R, -1)
+            lo = xl[a, rows].reshape(piece * R, -1)
             for x, w in ((h, wh), (lo, wh), (h, wl)):
                 e = jnp.dot(x, w[9 * l + i], preferred_element_type=F32)
                 d = e if d is None else d + e
-        raw[slot] = d
+        raw[slot, pl.ds(0, piece * R)] = d
 
     def finish(l, start, slot):
-        gain[pl.ds(start, PIECE)] = gelu(raw[slot] + bias[pl.ds(l, 1)]).reshape(PIECE, R, -1)
+        piece = PIECES[l]
+        g = gelu(raw[slot, pl.ds(0, piece * R)] + bias[pl.ds(l, 1)])
+        gain[pl.ds(start, piece)] = g.reshape(piece, R, -1)
+
+    def convolve(l, cols):
+        piece = PIECES[l]
+        pieces = (cols + piece - 1) // piece
+
+        def place(q):
+            return jnp.maximum(jnp.minimum(q * piece, cols - piece), 0)
+
+        def one(q, _):
+            finish(l, place(q - 1), (q + 1) % 2)
+            products(l, place(q), q % 2)
+            return 0
+
+        lax.fori_loop(0, pieces, one, 0)
+        finish(l, place(pieces - 1), (pieces + 1) % 2)
 
     c1, c2, c3 = 1, 3, 7
     n1, n2, n3 = total - 2, total - 6, total - 14
@@ -320,20 +338,10 @@
 
             l = jnp.where(p == k, layer, l)
             cols = jnp.where(p == k, placed(layer, segments)[1], cols)
-        s = jnp.where(l == 0, 1, jnp.where(l == 1, 2, jnp.where(l == 2, 4, 8)))
-
-        pieces = (cols + PIECE - 1) // PIECE
-
-        def place(q):
-            return jnp.maximum(jnp.minimum(q * PIECE, cols - PIECE), 0)
-
-        def one(q, _):
-            finish(l, place(q - 1), (q + 1) % 2)
-            chunk(l, s, place(q), q % 2)
-            return 0
-
-        lax.fori_loop(0, pieces, one, 0)
-        finish(l, place(pieces - 1), (pieces + 1) % 2)
+        for layer in range(4):
+            @pl.when(l == layer)
+            def _():
+                convolve(layer, cols)
         for k, (layer, segments, before) in enumerate(steps):
             @pl.when(p == k)
             def _():
@@ -365,7 +373,7 @@
             pltpu.VMEM((3, total, R, c), BF16),
             pltpu.VMEM((3, total, R, c), BF16),
             pltpu.VMEM((total, R, c), F32),
-            pltpu.VMEM((2, PIECE * R, c), F32),
+            pltpu.VMEM((2, max(PIECES) * R, c), F32),
             pltpu.VMEM((2, tiles, 8, LANES), F32),
             pltpu.VMEM((2, tiles, 8, LANES), F32),
             pltpu.SemaphoreType.DMA((4,)),

time: 84.5 us -> 82.7 us (0.979)
  Pallas kernels: 81 us -> 79.2 us
    pallas_call x1, Pallas kernels: 81 us -> 79.2 us  [local(): pl.pallas_call(functools.partial(kernel, ndev, n), out_shape=jax.ShapeDty...]
where the time goes in v4:
time: 82.7 us; the launch traced here: 82.5 us
  Pallas kernels  79.2 us (96%)
  local copies, waits for them, and re-layouts  2.11 us (3%)
  other arithmetic  1.24 us (1%)
    pallas_call x1, Pallas kernels, local(): pl.pallas_call(functools.partial(kernel, ndev, n), out_shape=jax.ShapeDty...  79.2 us
    unnamed x1, local copies, waits for them, and re-layouts  2.11 us

profile of v4, /device:TPU:0, one launch (start us, length us, event | category | flops | bytes accessed | tf_op | source)
XLA Modules:
  0.0 82.5 jit_solution(2854226381846235493)
XLA Ops:
  0.0 1.2 %convert_element_type.3 = f32[200]{0:T(256)} convert(s32[200]{0:T(256)} %param.7) | non-fusion elementwise | flops 200 | bytes 1600 | tf_op jit(solution)/shard_map/convert_element_type | solution.py:385
  1.2 79.2 %shard_map.55 = f32[52,16,200]{2,1,0:T(8,128)} custom-call(f32[52,16,200]{2,1,0:T(8,128)} %bitcast.7, f32[52,8,200]{2,1,0:T(8,128)} %bitcast.8, f32[1,200]{1,0:T(1,128)} %bitcast.9, f32[36,200,200]{2,1,0:T(8,128)} %bitcast.5, f32[4,200]{1,0:T(4,128)} %bias.1), custom_call_target="tpu_custom_call" | custom-call | tf_op jit(solution)/shard_map/pallas_call | solution.py:363
  80.4 2.1 %copy.7 = f32[16,52,200]{2,0,1:T(8,128)} copy(f32[16,52,200]{2,0,1:T(8,128)} %bitcast.6) | data formatting | bytes 1331200

commit v5 on v4

--- a/solution.py
+++ b/solution.py
@@ -270,12 +270,13 @@
         fold[0][0].wait()
         unpack(0, 0)
         start_all(upper)
-        start_all(fold[1])
+        fold[1][0].start()
 
     def upper_here():
         fold[0][1].wait()
         unpack(0, 1)
         wait_all(upper)
+        fold[1][1].start()
         north(0, 0)
         north(1, 0)
 

time: 82.7 us -> 81.7 us (0.988)
  Pallas kernels: 79.2 us -> 78.1 us
    pallas_call x1, Pallas kernels: 79.2 us -> 78.1 us  [local(): pl.pallas_call(functools.partial(kernel, ndev, n), out_shape=jax.ShapeDty...]
where the time goes in v5:
time: 81.7 us; the launch traced here: 81.5 us
  Pallas kernels  78.1 us (96%)
  local copies, waits for them, and re-layouts  2.11 us (3%)
  other arithmetic  1.24 us (2%)
    pallas_call x1, Pallas kernels, local(): pl.pallas_call(functools.partial(kernel, ndev, n), out_shape=jax.ShapeDty...  78.1 us
    unnamed x1, local copies, waits for them, and re-layouts  2.11 us

profile of v5, /device:TPU:0, one launch (start us, length us, event | category | flops | bytes accessed | tf_op | source)
XLA Modules:
  0.0 81.5 jit_solution(5503569057818616619)
XLA Ops:
  0.0 1.2 %convert_element_type.3 = f32[200]{0:T(256)} convert(s32[200]{0:T(256)} %param.7) | non-fusion elementwise | flops 200 | bytes 1600 | tf_op jit(solution)/shard_map/convert_element_type | solution.py:386
  1.2 78.1 %shard_map.55 = f32[52,16,200]{2,1,0:T(8,128)} custom-call(f32[52,16,200]{2,1,0:T(8,128)} %bitcast.7, f32[52,8,200]{2,1,0:T(8,128)} %bitcast.8, f32[1,200]{1,0:T(1,128)} %bitcast.9, f32[36,200,200]{2,1,0:T(8,128)} %bitcast.5, f32[4,200]{1,0:T(4,128)} %bias.1), custom_call_target="tpu_custom_call" | custom-call | tf_op jit(solution)/shard_map/pallas_call | solution.py:364
  79.4 2.1 %copy.7 = f32[16,52,200]{2,0,1:T(8,128)} copy(f32[16,52,200]{2,0,1:T(8,128)} %bitcast.6) | data formatting | bytes 1331200

commit v6 on v5

--- a/solution.py
+++ b/solution.py
@@ -12,7 +12,7 @@
 BF16 = jnp.bfloat16
 R = 16
 MOST = 8
-PIECES = (20, 19, 17, 26)
+PIECES = (20, 19, 34, 26)
 LANES = 128
 W = 15
 
@@ -123,12 +123,12 @@
             remote(south.at[pl.ds(n - W, W)], slab.at[0, 0, pl.ds(0, W), pl.ds(0, 8)], 4, right),
             remote(south.at[pl.ds(0, W)], slab.at[0, 0, pl.ds(W + n, W), pl.ds(0, 8)], 5, left)]
 
-    def onward(row, k):
-        rows = pl.ds(row, 8)
+    def onward(row, count, k):
+        rows = pl.ds(row, count)
         return [remote(slab.at[1, 0, pl.ds(n, W), rows], slab.at[1, 0, pl.ds(0, W), rows], k, left),
                 remote(slab.at[1, 0, pl.ds(W, W), rows], slab.at[1, 0, pl.ds(W + n, W), rows], k + 1, right)]
 
-    upper, lower = onward(16, 6), onward(8, 8)
+    upper, lower = onward(16, 8, 6), onward(9, 7, 8)
 
     own[0].wait()
     pack(0)

time: 81.7 us -> 81.5 us (level)
  no operation moved by 1% of the time
where the time goes in v6:
time: 81.5 us; the launch traced here: 81.4 us
  Pallas kernels  78 us (96%)
  local copies, waits for them, and re-layouts  2.11 us (3%)
  other arithmetic  1.24 us (2%)
    pallas_call x1, Pallas kernels, local(): pl.pallas_call(functools.partial(kernel, ndev, n), out_shape=jax.ShapeDty...  78 us
    unnamed x1, local copies, waits for them, and re-layouts  2.11 us

profile of v6, /device:TPU:0, one launch (start us, length us, event | category | flops | bytes accessed | tf_op | source)
XLA Modules:
  0.0 81.4 jit_solution(18385151502695515954)
XLA Ops:
  0.0 1.2 %convert_element_type.3 = f32[200]{0:T(256)} convert(s32[200]{0:T(256)} %param.7) | non-fusion elementwise | flops 200 | bytes 1600 | tf_op jit(solution)/shard_map/convert_element_type | solution.py:386
  1.2 78.0 %shard_map.55 = f32[52,16,200]{2,1,0:T(8,128)} custom-call(f32[52,16,200]{2,1,0:T(8,128)} %bitcast.7, f32[52,8,200]{2,1,0:T(8,128)} %bitcast.8, f32[1,200]{1,0:T(1,128)} %bitcast.9, f32[36,200,200]{2,1,0:T(8,128)} %bitcast.5, f32[4,200]{1,0:T(4,128)} %bias.1), custom_call_target="tpu_custom_call" | custom-call | tf_op jit(solution)/shard_map/pallas_call | solution.py:364
  79.3 2.1 %copy.7 = f32[16,52,200]{2,0,1:T(8,128)} copy(f32[16,52,200]{2,0,1:T(8,128)} %bitcast.6) | data formatting | bytes 1331200
